TPU v7x, 256 devices: a whole 4x4x8 slice. The times are simulated.
256 devices in a mesh: rows: 32 (over z_lo, y, core), rep: 8 (over x, z_hi).
Axes of the slice: x: 4, y: 4, z: 8 (z_hi: 2, z_lo: 4; z = z_hi * 4 + z_lo), core: 2. Of those that a mesh axis runs over, the one named last changes fastest.
Arguments:
- node_features: bfloat16 [65536, 256], P(('rows', 'rep')), may hold values from -6 to 6
- block_values: bfloat16 [256, 176, 128, 128], P(('rows', 'rep')), may hold values from -0.375 to 0.375
- block_rows: int32 [256, 176], P(('rows', 'rep')), may hold values from 0 to 15
- block_columns: int32 [256, 176], P(('rows', 'rep')), may hold values from 0 to 63
- block_used: int32 [256], P(('rows', 'rep')), may hold values from 23 to 176, as said below
- weight_self: bfloat16 [256, 128], replicated, may hold values from -0.375 to 0.375
- weight_message: bfloat16 [256, 128], replicated, may hold values from -0.375 to 0.375
- bias_hidden: float32 [128], replicated, may hold values from -3 to 3
- weight_output: bfloat16 [128, 256], replicated, may hold values from -0.5 to 0.5
- cotangent: bfloat16 [65536, 256], P(('rows', 'rep')), may hold values from -6 to 6
Outputs:
- updated: bfloat16 [65536, 256], P(('rows', 'rep'))
- grad_nodes: bfloat16 [65536, 256], P(('rows', 'rep'))
- grad_self: float32 [256, 128], replicated
- grad_message: float32 [256, 128], replicated
- grad_output: float32 [128, 256], replicated
- grad_bias: float32 [128], replicated
Inputs may be any that keep to these rules, and one draw needn't show every extreme that they name: `block_used`: in every draw some group has all 176 slots in use.
All inputs are finite; a program needn't handle non-finite values.
Results may differ from a plain program's by a relative error of at most 0.022.
Values may be sent and summed in bfloat16 or wider, within the bound.
A program may use at most 64 MiB of HBM per device.

v0:
```python
import math

import jax
import jax.numpy as jnp
from jax import lax
from jax.sharding import PartitionSpec as P

FEAT = 256
TILE = 128


def block_product(values, rows_of, cols_of, usable, source, target_count, transpose):
    size = math.gcd(values.shape[0], 64)
    count_groups = values.shape[0] // size
    width = source.shape[-1]
    stacked = (
        values.reshape(count_groups, size, TILE, TILE),
        rows_of.reshape(count_groups, size),
        cols_of.reshape(count_groups, size),
        usable.reshape(count_groups, size),
    )

    def one_group(totals, item):
        block_vals, rows_here, cols_here, usable_here = item
        if transpose:
            picked = source[rows_here]
            dest = cols_here
            product = jnp.einsum(
                "bji,bjf->bif", block_vals, picked, preferred_element_type=jnp.float32
            )
        else:
            picked = source[cols_here]
            dest = rows_here
            product = jnp.einsum(
                "bij,bjf->bif", block_vals, picked, preferred_element_type=jnp.float32
            )
        kept = jnp.where(usable_here[:, None, None], product, 0.0)
        return (totals.at[dest].add(kept), None)

    start = jnp.zeros((target_count, TILE, width), jnp.float32)
    totals, _ = lax.scan(one_group, start, stacked)
    return totals.reshape(target_count * TILE, width)


def body(
    node_features,
    block_values,
    block_rows,
    block_columns,
    block_used,
    weight_self,
    weight_message,
    bias_hidden,
    weight_output,
    cotangent,
):
    rows_count = lax.axis_size("rows")
    rep_count = lax.axis_size("rep")
    node_count = node_features.shape[0]
    brows_here = node_count * rep_count // TILE
    ctiles_here = node_count * rows_count // TILE
    values = block_values[0]
    rows_of = block_rows[0]
    cols_of = block_columns[0]
    usable = jnp.arange(values.shape[0], dtype=jnp.int32) < block_used[0]
    gathered = lax.all_gather(node_features, "rows", axis=0, tiled=True)
    column_tiles = gathered.reshape(ctiles_here, TILE, FEAT)
    partial_value = block_product(values, rows_of, cols_of, usable, column_tiles, brows_here, False)
    aggregated = lax.psum_scatter(
        partial_value.astype(jnp.bfloat16), "rep", scatter_dimension=0, tiled=True
    )
    pre = (
        jnp.dot(node_features, weight_self, preferred_element_type=jnp.float32)
        + jnp.dot(aggregated, weight_message, preferred_element_type=jnp.float32)
        + bias_hidden
    )
    hidden = jax.nn.silu(pre).astype(jnp.bfloat16)
    updated = (
        node_features.astype(jnp.float32)
        + jnp.dot(hidden, weight_output, preferred_element_type=jnp.float32)
    ).astype(jnp.bfloat16)
    hidden_grad = jnp.dot(cotangent, weight_output.T, preferred_element_type=jnp.float32)
    sigmoid_pre = jax.nn.sigmoid(pre)
    pre_grad = (hidden_grad * sigmoid_pre * (1.0 + pre * (1.0 - sigmoid_pre))).astype(jnp.bfloat16)
    term_self = jnp.dot(node_features.T, pre_grad, preferred_element_type=jnp.float32)
    term_message = jnp.dot(aggregated.T, pre_grad, preferred_element_type=jnp.float32)
    term_output = jnp.dot(hidden.T, cotangent, preferred_element_type=jnp.float32)
    term_bias = jnp.sum(pre_grad.astype(jnp.float32), axis=0)
    summed = lax.psum((term_self, term_message, term_output, term_bias), ("rows", "rep"))
    factor = 1.0 / math.sqrt(node_count * rows_count * rep_count)
    grad_self = summed[0] * factor
    grad_message = summed[1] * factor
    grad_output = summed[2] * factor
    grad_bias = summed[3] * factor
    message_grad = jnp.dot(pre_grad, weight_message.T, preferred_element_type=jnp.float32).astype(
        jnp.bfloat16
    )
    row_block = lax.all_gather(message_grad, "rep", axis=0, tiled=True).reshape(
        brows_here, TILE, FEAT
    )
    column_terms = block_product(values, rows_of, cols_of, usable, row_block, ctiles_here, True)
    transposed = lax.psum_scatter(
        column_terms.astype(jnp.bfloat16), "rows", scatter_dimension=0, tiled=True
    ).astype(jnp.float32)
    grad_nodes = (
        cotangent.astype(jnp.float32)
        + jnp.dot(pre_grad, weight_self.T, preferred_element_type=jnp.float32)
        + transposed
    ).astype(jnp.bfloat16)
    return (updated, grad_nodes, grad_self, grad_message, grad_output, grad_bias)


def solution(mesh):
    in_specs = (
        P(("rows", "rep"), None),
        P(("rows", "rep"), None, None, None),
        P(("rows", "rep"), None),
        P(("rows", "rep"), None),
        P(("rows", "rep")),
        P(),
        P(),
        P(),
        P(),
        P(("rows", "rep"), None),
    )
    out_specs = (P(("rows", "rep"), None), P(("rows", "rep"), None), P(), P(), P(), P())
    return jax.shard_map(body, mesh=mesh, in_specs=in_specs, out_specs=out_specs, check_vma=False)
```

profile of v0, /device:TPU:1, one launch (start us, length us, event | category | flops | bytes accessed | tf_op | source)
XLA Modules:
  0.0 731.4 jit_solution(11524882290295793573)
XLA Ops:
  12.0 65.0 %all-gather.3.cloned.1.call-done = bf16[8192,256]{1,0:T(8,128)(2,1)} async-done(((bf16[256,256]{1,0:T(8,128)(2,1)}), bf16[8192,256]{1,0:T(8,128)(2,1)}) %all-gather.3.cloned.1.call-update) | async-done | bytes 4194320 | tf_op jit(solution)/shard_map/all_gather | solution.py:66
  77.0 1.5 broadcast_in_dim.37
  78.6 96.0 %while.20 = (s32[]{:T(128)}, f32[16,128,256]{2,1,0:T(8,128)}, s32[11,16]{1,0:T(8,128)S(1)}, pred[11,16]{1,0:T(8,128)(4,1)S(1)}, bf16[11,16,128,128]{3,2,1,0:T(8,...) while((s32[]{:T(128)}, f32[16,128,256]{2,1,0:T(8,128)}, ...), condition=%wide.region_2.3_spmd, body=%wide.region_0.2_spmd.sunk | while | flops 135267424 | bytes 12063321 | solution.py:41
  78.6 2.8 gather_fusion
  82.9 4.4 scatter_fusion
  87.3 2.8 gather_fusion
  91.6 4.3 scatter_fusion
  95.9 2.8 gather_fusion
  100.2 4.5 scatter_fusion
  104.7 2.8 gather_fusion
  109.0 4.5 scatter_fusion
  113.6 2.8 gather_fusion
  117.9 4.3 scatter_fusion
  122.2 2.8 gather_fusion
  125.1 1.5 convolution_select_fusion.4
  126.5 4.4 scatter_fusion
  131.0 2.8 gather_fusion
  135.3 4.4 scatter_fusion
  139.6 2.8 gather_fusion
  143.9 4.4 scatter_fusion
  148.4 2.8 gather_fusion
  151.2 1.5 convolution_select_fusion.4
  152.7 4.4 scatter_fusion
  157.1 2.8 gather_fusion
  161.4 4.4 scatter_fusion
  165.9 2.8 gather_fusion
  168.7 1.5 convolution_select_fusion.4
  170.2 4.4 scatter_fusion
  174.6 2.7 convert_element_type.40
  177.6 83.4 %reduce-scatter.3.cloned.1.call-done = bf16[256,256]{1,0:T(8,128)(2,1)} async-done(((bf16[2048,256]{1,0:T(8,128)(2,1)}), bf16[256,256]{1,0:T(8,128)(2,1)}) %reduce-scatter.3.cloned.1.call-update) | async-done | bytes 131088 | tf_op jit(solution)/shard_map/reduce_scatter | solution.py:69
  263.3 8.1 %copy.16 = bf16[1,176,128,128]{2,3,1,0:T(8,128)(2,1)} copy(bf16[1,176,128,128]{3,2,1,0:T(8,128)(2,1)} %bitcast.92) | data formatting | bytes 11534336 | tf_op args[1]
  274.1 48.5 %all-gather.5.cloned.1.call-done = bf16[2048,256]{1,0:T(8,128)(2,1)} async-done(((bf16[256,256]{1,0:T(8,128)(2,1)}), bf16[2048,256]{1,0:T(8,128)(2,1)}) %all-gather.5.cloned.1.call-update) | async-done | bytes 1048592 | tf_op jit(solution)/shard_map/all_gather | solution.py:98
  322.6 4.3 broadcast_in_dim.38
  326.9 87.1 %while.21 = (s32[]{:T(128)}, f32[64,128,256]{2,1,0:T(8,128)}, s32[11,16]{1,0:T(8,128)S(1)}, pred[11,16]{1,0:T(8,128)(4,1)S(1)}, bf16[11,16,128,128]{2,3,1,0:T(8,...) while((s32[]{:T(128)}, f32[64,128,256]{2,1,0:T(8,128)}, ...), condition=%wide.region_6.7_spmd, body=%wide.region_4.6_spmd.sunk | while | flops 135267424 | bytes 12063321 | solution.py:41
  326.9 1.8 gather_fusion.1
  330.2 4.6 scatter_fusion.1
  334.8 1.8 gather_fusion.1
  338.2 4.5 scatter_fusion.1
  342.7 1.8 gather_fusion.1
  346.0 4.6 scatter_fusion.1
  350.6 1.8 gather_fusion.1
  354.0 4.5 scatter_fusion.1
  358.5 1.8 gather_fusion.1
  360.4 1.5 convolution_select_fusion.5
  361.9 4.6 scatter_fusion.1
  366.4 1.8 gather_fusion.1
  369.8 4.5 scatter_fusion.1
  374.3 1.8 gather_fusion.1
  376.2 1.5 convolution_select_fusion.5
  377.6 4.6 scatter_fusion.1
  382.2 1.8 gather_fusion.1
  385.6 4.6 scatter_fusion.1
  390.2 1.8 gather_fusion.1
  393.5 4.6 scatter_fusion.1
  398.1 1.8 gather_fusion.1
  401.4 4.6 scatter_fusion.1
  406.0 1.8 gather_fusion.1
  409.4 4.6 scatter_fusion.1
  414.0 6.0 convert_element_type.47
  420.0 75.5 %psum.31 = f32[128]{0:T(128)S(1)} all-reduce(f32[128]{0:T(128)S(1)} %get-tuple-element.130), channel_id=1, replica_groups=mesh['rows'=32,'rep'=8] {'rows','rep'}, use_global_device_ids=true, to_apply=%region_12.13 | all-reduce | flops 128 | bytes 1024 | tf_op jit(solution)/shard_map/psum | solution.py:89
  496.9 79.6 %all-reduce.3.cloned.1.call-done = (f32[256,128]{0,1:T(8,128)}, f32[256,128]{0,1:T(8,128)}, f32[128,256]{1,0:T(8,128)}) async-done(((f32[256,128]{0,1:T(8,128)}, f32[256,128]{0,1:T(8,128)}, f32[128,256]{1,0:T(8,128)}), (f32[256,128]{0,1:T(8,128)}, f32[256,128]{0,1:T(8,128)}, f32[128,256]{1,0:T(8,128)})) %all-reduce.3.cloned.1.call-update) | async-done | bytes 393232 | tf_op jit(solution)/shard_map/psum | solution.py:89
  579.0 1.6 broadcast_multiply_fusion
  580.6 142.5 %reduce-scatter.5.cloned.1.call-done = bf16[256,256]{1,0:T(8,128)(2,1)} async-done(((bf16[8192,256]{1,0:T(8,128)(2,1)}), bf16[256,256]{1,0:T(8,128)(2,1)}) %reduce-scatter.5.cloned.1.call-update) | async-done | bytes 131088 | tf_op jit(solution)/shard_map/reduce_scatter | solution.py:102
  723.1 1.8 fusion.16
  (131 shorter events, 38.7 us)
Async XLA Ops:
  7.2 254.9 %copy-start = (bf16[128,256]{1,0:T(8,128)(2,1)S(1)}, bf16[128,256]{1,0:T(8,128)(2,1)}, u32[]{:S(2)}) copy-start(bf16[128,256]{1,0:T(8,128)(2,1)} %param.22) | copy-start | bytes 196612
  7.2 69.8 %all-gather.3.cloned.1.call-start = ((), (), s32[]{:S(2)}) async-start(), calls=%async_computation.2 | async-start | bytes 4325376 | tf_op jit(solution)/shard_map/all_gather | solution.py:66
  7.9 253.1 %reduce-scatter.3.cloned.1.call-start = ((), (), s32[]{:S(2)}) async-start(), calls=%async_computation.3 | async-start | bytes 1179648 | tf_op jit(solution)/shard_map/reduce_scatter | solution.py:69
  174.6 2.8 copy-start.1
  174.6 2.9 copy-start.4
  174.6 86.5 %copy-start.3 = (bf16[256,128]{1,0:T(8,128)(2,1)S(1)}, bf16[256,128]{1,0:T(8,128)(2,1)}, u32[]{:S(2)}) copy-start(bf16[256,128]{1,0:T(8,128)(2,1)} %param.20) | copy-start | bytes 196612
  174.6 86.5 %copy-start.9 = (f32[128]{0:T(128)S(1)}, f32[128]{0:T(128)}, u32[]{:S(2)}) copy-start(f32[128]{0:T(128)} %param.21) | copy-start | bytes 1540
  174.6 87.5 %copy-start.5 = (bf16[256,256]{1,0:T(8,128)(2,1)S(1)}, bf16[256,256]{1,0:T(8,128)(2,1)}, u32[]{:S(2)}) copy-start(bf16[256,256]{1,0:T(8,128)(2,1)} %param.23) | copy-start | bytes 393220
  177.3 145.3 %all-gather.5.cloned.1.call-start = ((), (), s32[]{:S(2)}) async-start(), calls=%async_computation.4 | async-start | bytes 1179648 | tf_op jit(solution)/shard_map/all_gather | solution.py:98
  262.1 11.0 %copy-start.7 = (f32[256,128]{1,0:T(8,128)}, f32[256,128]{1,0:T(8,128)S(1)}, u32[]{:S(2)}) copy-start(f32[256,128]{1,0:T(8,128)S(1)} %fusion.17) | copy-start | bytes 393220
  263.2 9.0 %copy-start.2 = (bf16[256,256]{1,0:T(8,128)(2,1)S(1)}, bf16[256,256]{1,0:T(8,128)(2,1)}, u32[]{:S(2)}) copy-start(bf16[256,256]{1,0:T(8,128)(2,1)} %reduce-scatter.3.cloned.1.call-done) | copy-start | bytes 393220
  263.2 313.3 %all-reduce.3.cloned.1.call-start = ((), (), s32[]{:S(2)}) async-start(), calls=%async_computation.6 | async-start | bytes 786432 | tf_op jit(solution)/shard_map/psum | solution.py:89
  274.1 449.0 %reduce-scatter.5.cloned.1.call-start = ((), (), s32[]{:S(2)}) async-start(), calls=%async_computation.5 | async-start | bytes 4325376 | tf_op jit(solution)/shard_map/reduce_scatter | solution.py:102
  420.0 76.1 %copy-start.8 = (f32[256,128]{1,0:T(8,128)S(1)}, f32[256,128]{1,0:T(8,128)}, u32[]{:S(2)}) copy-start(f32[256,128]{1,0:T(8,128)} %copy-done.7) | copy-start | bytes 393220
  420.0 303.1 %copy-start.6 = (bf16[256,256]{1,0:T(8,128)(2,1)S(1)}, bf16[256,256]{1,0:T(8,128)(2,1)}, u32[]{:S(2)}) copy-start(bf16[256,256]{1,0:T(8,128)(2,1)} %param.23) | copy-start | bytes 393220
Sparse Core Ops, SparseCore 0:
  9.9 67.1 all-gather.2
  177.5 83.4 reduce-scatter.2
  264.6 58.0 all-gather.4
  330.0 246.4 all-reduce.2
  579.1 144.0 reduce-scatter.4
where the time goes:
time: 739 us; the launch traced here: 731 us
  waiting for transfers between devices  420 us (57%)
  other arithmetic  113 us (15%)
  blocking collectives  75.5 us (10%)
  local copies, waits for them, and re-layouts  67.6 us (9%)
  matrix products  39.8 us (5%)
  between operations  14.5 us (2%)
    reduce_scatter x1, waiting for transfers between devices, body(): lax.psum_scatter(column_terms.astype(jnp.bfloat16), 'rows', scatter_dimen...  143 us
    scatter-add x22, other arithmetic, one_group(): return (totals.at[dest].add(kept), None)  98.5 us
    reduce_scatter x1, waiting for transfers between devices, body(): lax.psum_scatter(partial_value.astype(jnp.bfloat16), 'rep', scatter_dimen...  83.4 us
    psum x1, waiting for transfers between devices, body(): lax.psum((term_self, term_message, term_output, term_bias), ('rows', 'rep'))  79.6 us
    psum x1, blocking collectives, body(): lax.psum((term_self, term_message, term_output, term_bias), ('rows', 'rep'))  75.5 us
    all_gather x1, waiting for transfers between devices, body(): gathered = lax.all_gather(node_features, 'rows', axis=0, tiled=True)  65 us
    all_gather x1, waiting for transfers between devices, body(): lax.all_gather(message_grad, 'rep', axis=0, tiled=True)  48.5 us
    gather x11, local copies, waits for them, and re-layouts, one_group(): picked = source[cols_here]  30.8 us
  transfers between devices with their start and end apart: 5, of which 5 were waited for; matrix products, arithmetic and copies ran while one was open for 16% of the time, Pallas kernels for 0%

commit v1 on v0

v1 whole, which is shorter than its diff:
```python
import functools
import math

import jax
import jax.numpy as jnp
from jax import lax
from jax.experimental import pallas as pl
from jax.experimental.pallas import tpu as pltpu
from jax.sharding import PartitionSpec as P

FEAT = 256
HID = 128
TILE = 128
NBLK = 176
NB_PAD = 256
BROWS = 16
CTILES = 64
ZERO_SLOT = NBLK
MESH = pl.DeviceIdType.MESH
F32 = jnp.float32
BF16 = jnp.bfloat16
UNROLL = 8
SELF_ROWS = 24
MSG_ROWS = 8


def dot(a, b, dims=((1,), (0,))):
    return lax.dot_general(a, b, (dims, ((), ())), preferred_element_type=F32)


def kernel(
    used_ref, x_ref, values_ref, brow_ref, bcol_ref, ws_ref, wm_ref, bias_ref, wo_ref, cot_ref,
    updated_ref, gnodes_ref, gself_ref, gmsg_ref, gout_ref, gbias_ref,
    vals, gath, xgath, runs, idx_v, idx_s, ident, base, hgrad,
    part_send, recv_a, recv_b, zsend, recv_z, pgt,
    t_send, recv_c, y_send, recv_y, z7_send, recv_z7,
    m_a, m_a_recv, m_a_in, m_a_rep, m_a_fin,
    m_b, m_b_recv, m_b_in, m_b_rep, m_b_fin,
    v_sem, i_sem, send_sems, p1z, p1y, p1c, xgz, xgy, xgc,
    r3a, r3b, r3z, r5x, r5z, r5f, r7c, r7y, r7z,
    aa_c, aa_in, aa_rep, aa_out, aa_f, ab_c, ab_in, ab_rep, ab_out, ab_f,
):
    row = lax.axis_index("rows")
    rep = lax.axis_index("rep")
    zl, y, c = row // 8, (row // 2) % 4, row % 2
    x, zh = rep // 2, rep % 2
    oc, ozh = 1 - c, 1 - zh

    def dev(zl_=None, y_=None, c_=None, x_=None, zh_=None):
        zl_ = zl if zl_ is None else zl_
        y_ = y if y_ is None else y_
        c_ = c if c_ is None else c_
        x_ = x if x_ is None else x_
        zh_ = zh if zh_ is None else zh_
        return {"rows": zl_ * 8 + y_ * 2 + c_, "rep": x_ * 2 + zh_}

    def around(i, d):
        return (i + d) % 4

    near = (1, 3, 2)
    sibling = dev(c_=oc)
    partner = dev(zh_=ozh)
    partners = [sibling, partner]
    for d in near:
        partners += [dev(y_=around(y, d)), dev(zl_=around(zl, d)), dev(x_=around(x, d))]
    barrier = pltpu.get_barrier_semaphore()
    for p in partners:
        pl.semaphore_signal(barrier, inc=1, device_id=p, device_id_type=MESH)

    load_values = pltpu.make_async_copy(values_ref.at[0], vals, v_sem)
    load_values.start()

    sent = []

    def send(src, dst, recv, to):
        copy = pltpu.make_async_remote_copy(
            src_ref=src, dst_ref=dst, send_sem=send_sems.at[len(sent)], recv_sem=recv,
            device_id=to, device_id_type=MESH,
        )
        copy.start()
        sent.append(copy)

    def arrived(dst, recv):
        pltpu.make_async_remote_copy(
            src_ref=dst, dst_ref=dst, send_sem=send_sems.at[0], recv_sem=recv,
            device_id=sibling, device_id_type=MESH,
        ).wait_recv()

    def shard(c_, y_, zl_):
        return gath.at[pl.ds((c_ * 16 + y_ * 4 + zl_) * 2, 2)]

    def xshards(c_, y_, zl_, n):
        return xgath.at[pl.ds(c_ * 16 + y_ * 4 + zl_, n)]

    feats = x_ref[...]
    mine = c * 16 + y * 4 + zl
    gath[pl.ds(mine * 2, 2)] = dot(feats, wm_ref[...]).astype(BF16).reshape(2, TILE, HID)
    xgath[mine] = feats
    pl.semaphore_wait(barrier, len(partners))
    own = shard(c, y, zl)
    for d in near:
        send(own, own, p1z.at[zl], dev(zl_=around(zl, d)))
    for d in near:
        send(own, own, p1y.at[y, zl], dev(y_=around(y, d)))
    send(own, own, p1c.at[y, zl], sibling)

    used = used_ref[0]
    idx_v[...] = jnp.zeros_like(idx_v)
    idx_v[0:1, 0:NBLK] = brow_ref[...]
    idx_v[1:2, 0:NBLK] = bcol_ref[...]
    lane = lax.broadcasted_iota(jnp.int32, (1, NB_PAD), 1)
    lanes = lax.broadcasted_iota(jnp.int32, (NB_PAD, NB_PAD), 1)
    usable = lane < used
    rows_of = idx_v[0:1, :]
    cols_of = idx_v[1:2, :]
    source = cols_of >> 1
    tile_of = (((source & 1) * 16 + ((source >> 1) & 3) * 4 + (source >> 3)) << 1) + (cols_of & 1)

    def listing(key, other):
        packed = (((key << 8) + lane) << 7) + other
        along = jnp.broadcast_to(packed, (NB_PAD, NB_PAD))
        down = along.T
        rank = jnp.sum((along < down).astype(jnp.int32), axis=1, keepdims=True)
        ordered = jnp.sum(jnp.where(rank == lanes, down, 0), axis=0, keepdims=True)
        keys = down >> 15
        upto = jnp.sum((keys <= lanes).astype(jnp.int32), axis=0, keepdims=True)
        below = jnp.sum((keys < lanes).astype(jnp.int32), axis=0, keepdims=True)
        return ordered, jnp.where(upto > below, upto - 1, ZERO_SLOT)

    order_f, end_f = listing(jnp.where(usable, rows_of, BROWS), tile_of)
    order_b, end_b = listing(jnp.where(usable, tile_of, CTILES), rows_of)
    idx_v[0:1, :] = order_f
    idx_v[1:2, :] = end_f
    idx_v[2:3, :] = order_b
    idx_v[3:4, :] = end_b
    load_index = pltpu.make_async_copy(idx_v, idx_s, i_sem)
    load_index.start()

    for d in near:
        zs = around(zl, d)
        arrived(shard(c, y, zs), p1z.at[zs])
        for e in near:
            send(shard(c, y, zs), shard(c, y, zs), p1y.at[y, zs], dev(y_=around(y, e)))
        send(shard(c, y, zs), shard(c, y, zs), p1c.at[y, zs], sibling)
    for d in near:
        send(xshards(c, y, zl, 1), xshards(c, y, zl, 1), xgz.at[zl], dev(zl_=around(zl, d)))

    ident[...] = dot(feats, ws_ref[...]) + bias_ref[...]
    cot = cot_ref[...]
    hgrad[...] = dot(cot, wo_ref[...], ((1,), (1,)))
    runs[ZERO_SLOT] = jnp.zeros((TILE, HID), F32)

    for zd in (0,) + near:
        zs = around(zl, zd)
        for e in near:
            ys = around(y, e)
            arrived(shard(c, ys, zs), p1y.at[ys, zs])
            send(shard(c, ys, zs), shard(c, ys, zs), p1c.at[ys, zs], sibling)
    for yd in range(4):
        for zd in range(4):
            arrived(shard(oc, yd, zd), p1c.at[yd, zd])
    load_values.wait()
    load_index.wait()

    for d in near:
        zs = around(zl, d)
        arrived(xshards(c, y, zs, 1), xgz.at[zs])
    for e in near:
        send(xshards(c, y, 0, 4), xshards(c, y, 0, 4), xgy.at[y], dev(y_=around(y, e)))

    def products(which, pick):
        def step(i, carry):
            total, before = carry
            for u in range(UNROLL):
                p = i * UNROLL + u
                word = idx_s[which, p]
                key = word >> 15
                term = pick((word >> 7) & 255, word & 127)
                total = jnp.where(key == before, total, 0.0) + term
                runs[p] = total
                before = key
            return total, before

        lax.fori_loop(0, NBLK // UNROLL, step, (jnp.zeros((TILE, HID), F32), jnp.int32(-1)))

    products(0, lambda b, o: dot(vals[b], gath[o]))

    def part(j, k):
        return runs[idx_s[1, j * 2 + k]]

    for zz, recv_sems, recv in ((ozh, r3a, recv_a), (zh, r3b, recv_b)):
        for d in near:
            xs = around(x, d)
            j = xs * 2 + zz
            for k in range(2):
                part_send[j, k] = part(j, k).astype(BF16)
            send(part_send.at[j], recv.at[x], recv_sems.at[x], dev(x_=xs))
    for d in near:
        xs = around(x, d)
        arrived(recv_a.at[xs], r3a.at[xs])
    for k in range(2):
        total = part(x * 2 + ozh, k)
        for d in near:
            total = total + recv_a[around(x, d), k].astype(F32)
        zsend[k] = total.astype(BF16)
    send(zsend, recv_z, r3z.at[0], partner)
    for d in near:
        xs = around(x, d)
        arrived(recv_b.at[xs], r3b.at[xs])
    agg = []
    for k in range(2):
        total = part(x * 2 + zh, k)
        for d in near:
            total = total + recv_b[around(x, d), k].astype(F32)
        agg.append(total)
    arrived(recv_z, r3z.at[0])
    hidden, pgrad = [], []
    for k in range(2):
        here = pl.ds(k * TILE, TILE)
        pre = ident[here, :] + (agg[k] + recv_z[k].astype(F32))
        sig = jax.nn.sigmoid(pre)
        hidden.append((pre * sig).astype(BF16))
        grad = hgrad[here, :] * sig * (1.0 + pre * (1.0 - sig))
        pgrad.append(grad.astype(BF16))
        pgt[rep, k] = grad.T.astype(BF16)

    send(pgt.at[rep], pgt.at[rep], r5z.at[0], partner)
    for d in near:
        send(pgt.at[rep], pgt.at[rep], r5x.at[x], dev(x_=around(x, d)))
    hid = jnp.concatenate(hidden, axis=0)
    pg = jnp.concatenate(pgrad, axis=0)
    for e in near:
        ys = around(y, e)
        arrived(xshards(c, ys, 0, 4), xgy.at[ys])
    send(xshards(c, 0, 0, 16), xshards(c, 0, 0, 16), xgc.at[0], sibling)
    updated_ref[...] = (feats.astype(F32) + dot(hid, wo_ref[...])).astype(BF16)
    base[...] = cot.astype(F32) + dot(pg, ws_ref[...], ((1,), (1,)))
    term_self = dot(feats, pg, ((0,), (0,)))
    term_out = dot(hid, cot, ((0,), (0,)))
    term_bias = jnp.sum(pg.astype(F32).reshape(32, 8, HID), axis=0)
    for cc in range(2):
        m_a[cc, :, 0:8, :] = term_self[cc * 128:(cc + 1) * 128, :].reshape(16, 8, HID)
        m_a[cc, :, 8:16, :] = term_out[:, cc * 128:(cc + 1) * 128].reshape(16, 8, HID)
        m_a[cc, :, 16:24, :] = jnp.broadcast_to(term_bias[None], (16, 8, HID))

    spot = zl * 4 + y
    far = [(a, b) for a in range(4) for b in range(4) if (a, b) != (0, 0)]

    def grads_core(m, m_recv, sem):
        send(m.at[oc], m_recv, sem.at[0], sibling)

    def grads_rows(m, m_recv, m_in, sem_c, sem):
        arrived(m_recv, sem_c.at[0])
        m_recv[...] = m_recv[...] + m[c]
        m_in[spot] = m_recv[spot]
        for a, b in far:
            zt, yt = around(zl, a), around(y, b)
            send(m_recv.at[zt * 4 + yt], m_in.at[spot], sem.at[spot], dev(zl_=zt, y_=yt))

    def grads_rep(m_in, m_rep, sem_in, sem):
        for a, b in far:
            q = around(zl, a) * 4 + around(y, b)
            arrived(m_in.at[q], sem_in.at[q])
        total = m_in[0]
        for q in range(1, 16):
            total = total + m_in[q]
        m_rep[rep] = total
        for d in range(1, 8):
            j = (rep + d) % 8
            send(m_rep.at[rep], m_rep.at[rep], sem.at[rep], dev(x_=j // 2, zh_=j % 2))

    def grads_out(m_rep, m_fin, sem_rep, sem):
        for d in range(1, 8):
            j = (rep + d) % 8
            arrived(m_rep.at[j], sem_rep.at[j])
        total = m_rep[0]
        for j in range(1, 8):
            total = total + m_rep[j]
        m_fin[c, spot] = total
        for a, b in far:
            zt, yt = around(zl, a), around(y, b)
            send(m_fin.at[c, spot], m_fin.at[c, spot], sem.at[spot], dev(zl_=zt, y_=yt))

    def grads_last(m_fin, sem_out, sem_f):
        for a, b in far:
            q = around(zl, a) * 4 + around(y, b)
            arrived(m_fin.at[c, q], sem_out.at[q])
        send(m_fin.at[c], m_fin.at[c], sem_f.at[0], sibling)

    grads_core(m_a, m_a_recv, aa_c)
    oj = x * 2 + ozh
    arrived(pgt.at[oj], r5z.at[0])
    for d in near:
        send(pgt.at[oj], pgt.at[oj], r5f.at[x], dev(x_=around(x, d)))
    grads_rows(m_a, m_a_recv, m_a_in, aa_c, aa_in)
    for d in near:
        xs = around(x, d)
        arrived(pgt.at[xs * 2 + zh], r5x.at[xs])
        arrived(pgt.at[xs * 2 + ozh], r5f.at[xs])

    products(2, lambda b, o: dot(pgt[o >> 1, o & 1], vals[b]))

    grads_rep(m_a_in, m_a_rep, aa_in, aa_rep)

    def column(t):
        return runs[idx_s[3, t]]

    def convert(t, _):
        t_send[t] = column(t).astype(BF16)
        return 0

    for ys in range(4):
        lax.fori_loop(oc * 32 + ys * 8, oc * 32 + ys * 8 + 8, convert, 0)
        send(t_send.at[pl.ds(oc * 32 + ys * 8, 8)], recv_c.at[ys], r7c.at[ys], sibling)
    lax.fori_loop(c * 32, c * 32 + 32, convert, 0)
    arrived(xshards(oc, 0, 0, 16), xgc.at[0])

    def message(i, total):
        for u in range(2):
            s = i * 2 + u
            for k in range(2):
                total = total + dot(t_send[s * 2 + k], xgath[s, k * TILE:(k + 1) * TILE, :])
        return total

    term_msg = lax.fori_loop(0, 16, message, jnp.zeros((HID, FEAT), F32))
    m_b[...] = term_msg.T.reshape(2, 16, 8, HID)
    grads_core(m_b, m_b_recv, ab_c)

    for d in near + (0,):
        ys = around(y, d)
        arrived(recv_c.at[ys], r7c.at[ys])
        for t in range(8):
            y_send[ys, t] = (column(c * 32 + ys * 8 + t) + recv_c[ys, t].astype(F32)).astype(BF16)
        if d:
            send(y_send.at[ys], recv_y.at[y], r7y.at[y], dev(y_=ys))
    grads_rows(m_b, m_b_recv, m_b_in, ab_c, ab_in)
    grads_out(m_a_rep, m_a_fin, aa_rep, aa_out)
    for d in near:
        ys = around(y, d)
        arrived(recv_y.at[ys], r7y.at[ys])
    final = []
    for d in near + (0,):
        zs = around(zl, d)
        for k in range(2):
            total = y_send[y, zs * 2 + k].astype(F32)
            for e in near:
                total = total + recv_y[around(y, e), zs * 2 + k].astype(F32)
            if d:
                z7_send[zs, k] = total.astype(BF16)
            else:
                final.append(total)
        if d:
            send(z7_send.at[zs], recv_z7.at[zl], r7z.at[zl], dev(zl_=zs))
    grads_rep(m_b_in, m_b_rep, ab_in, ab_rep)
    grads_last(m_a_fin, aa_out, aa_f)
    for d in near:
        zs = around(zl, d)
        arrived(recv_z7.at[zs], r7z.at[zs])
    for k in range(2):
        total = final[k]
        for d in near:
            total = total + recv_z7[around(zl, d), k].astype(F32)
        here = pl.ds(k * TILE, TILE)
        gnodes_ref[here, :] = (
            base[here, :] + dot(total.T.astype(BF16), wm_ref[...], ((1,), (1,)))
        ).astype(BF16)

    grads_out(m_b_rep, m_b_fin, ab_rep, ab_out)
    grads_last(m_b_fin, ab_out, ab_f)
    arrived(m_a_fin.at[oc], aa_f.at[0])
    factor = 1.0 / math.sqrt(65536)
    for cc in range(2):
        rows_here = slice(cc * 128, (cc + 1) * 128)
        gself_ref[rows_here, :] = m_a_fin[cc, :, 0:8, :].reshape(128, HID) * factor
        gout_ref[:, rows_here] = m_a_fin[cc, :, 8:16, :].reshape(128, HID) * factor
    gbias_ref[...] = jnp.sum(m_a_fin[0, 0, 16:24, :], axis=0, keepdims=True) * factor
    arrived(m_b_fin.at[oc], ab_f.at[0])
    gmsg_ref[...] = m_b_fin[...].reshape(FEAT, HID) * factor
    for copy in sent:
        copy.wait_send()


def body(x, values, brow, bcol, used, ws, wm, bias, wo, cot):
    vmem = pl.BlockSpec(memory_space=pltpu.VMEM)
    dma = pltpu.SemaphoreType.DMA

    def pieces(n):
        return [
            pltpu.VMEM((2, 16, n, HID), F32),
            pltpu.VMEM((16, n, HID), F32),
            pltpu.VMEM((16, n, HID), F32),
            pltpu.VMEM((8, n, HID), F32),
            pltpu.VMEM((2, 16, n, HID), F32),
        ]

    grad_sems = [dma((1,)), dma((16,)), dma((8,)), dma((16,)), dma((1,))]
    updated, gnodes, gself, gmsg, gout, gbias = pl.pallas_call(
        kernel,
        out_shape=(
            jax.ShapeDtypeStruct((256, FEAT), BF16),
            jax.ShapeDtypeStruct((256, FEAT), BF16),
            jax.ShapeDtypeStruct((FEAT, HID), F32),
            jax.ShapeDtypeStruct((FEAT, HID), F32),
            jax.ShapeDtypeStruct((HID, FEAT), F32),
            jax.ShapeDtypeStruct((1, HID), F32),
        ),
        in_specs=[pl.BlockSpec(memory_space=pltpu.SMEM), vmem, pl.BlockSpec(memory_space=pl.ANY)] + [vmem] * 7,
        out_specs=(vmem,) * 6,
        scratch_shapes=[
            pltpu.VMEM((NBLK, TILE, TILE), BF16),
            pltpu.VMEM((CTILES, TILE, HID), BF16),
            pltpu.VMEM((32, 256, FEAT), BF16),
            pltpu.VMEM((NBLK + 1, TILE, HID), F32),
            pltpu.VMEM((8, NB_PAD), jnp.int32),
            pltpu.SMEM((8, NB_PAD), jnp.int32),
            pltpu.VMEM((256, HID), F32),
            pltpu.VMEM((256, FEAT), F32),
            pltpu.VMEM((256, HID), F32),
            pltpu.VMEM((8, 2, TILE, HID), BF16),
            pltpu.VMEM((4, 2, TILE, HID), BF16),
            pltpu.VMEM((4, 2, TILE, HID), BF16),
            pltpu.VMEM((2, TILE, HID), BF16),
            pltpu.VMEM((2, TILE, HID), BF16),
            pltpu.VMEM((8, 2, HID, TILE), BF16),
            pltpu.VMEM((CTILES, HID, TILE), BF16),
            pltpu.VMEM((4, 8, HID, TILE), BF16),
            pltpu.VMEM((4, 8, HID, TILE), BF16),
            pltpu.VMEM((4, 8, HID, TILE), BF16),
            pltpu.VMEM((4, 2, HID, TILE), BF16),
            pltpu.VMEM((4, 2, HID, TILE), BF16),
            *pieces(SELF_ROWS),
            *pieces(MSG_ROWS),
            dma, dma, dma((160,)),
            dma((4,)), dma((4, 4)), dma((4, 4)), dma((4,)), dma((4,)), dma((1,)),
            dma((4,)), dma((4,)), dma((1,)), dma((4,)), dma((1,)), dma((4,)),
            dma((4,)), dma((4,)), dma((4,)),
            *grad_sems,
            *grad_sems,
        ],
        compiler_params=pltpu.CompilerParams(
            collective_id=0, has_side_effects=True, vmem_limit_bytes=52 * 2**20
        ),
        name="layer",
    )(used, x, values, brow, bcol, ws, wm, bias.reshape(1, HID), wo, cot)
    return updated, gnodes, gself, gmsg, gout, gbias.reshape(HID)


def solution(mesh):
    sharded = P(("rows", "rep"), None)
    in_specs = (
        sharded, P(("rows", "rep"), None, None, None), sharded, sharded, P(("rows", "rep")),
        P(), P(), P(), P(), sharded,
    )
    out_specs = (sharded, sharded, P(), P(), P(), P())
    return jax.shard_map(body, mesh=mesh, in_specs=in_specs, out_specs=out_specs, check_vma=False)
```

time: 739 us -> 115 us (0.16)
  waiting for transfers between devices: 420 us -> 0 us
  other arithmetic: 113 us -> 0 us
  Pallas kernels: 0 us -> 103 us
  blocking collectives: 75.5 us -> 0 us
  local copies, waits for them, and re-layouts: 67.6 us -> 10.1 us
  matrix products: 39.8 us -> 0 us
  between operations: 14.5 us -> 1.31 us
    reduce_scatter x2 -> x0, waiting for transfers between devices: 226 us -> none  [the longest x1 143 us: body(): lax.psum_scatter(column_terms.astype(jnp.bfloat16), 'rows', scatter_dimen...]
    all_gather x2 -> x0, waiting for transfers between devices: 114 us -> none  [the longest x1 65 us: body(): gathered = lax.all_gather(node_features, 'rows', axis=0, tiled=True)]
    pallas_call x0 -> x1, Pallas kernels: none -> 103 us  [body(): pl.pallas_call(kernel, out_shape=(jax.ShapeDtypeStruct((256, FEAT), BF16)...]
    scatter-add x22 -> x0, other arithmetic: 98.5 us -> none  [one_group(): return (totals.at[dest].add(kept), None)]
    psum x1 -> x0, waiting for transfers between devices: 79.6 us -> none  [body(): lax.psum((term_self, term_message, term_output, term_bias), ('rows', 'rep'))]
    psum x1 -> x0, blocking collectives: 75.5 us -> none  [body(): lax.psum((term_self, term_message, term_output, term_bias), ('rows', 'rep'))]
    gather x22 -> x0, local copies, waits for them, and re-layouts: 51.1 us -> none  [the longest x11 30.8 us: one_group(): picked = source[cols_here]]
    dot_general x31 -> x0, matrix products: 39.8 us -> none  [the longest x11 16.1 us: one_group(): jnp.einsum('bij,bjf->bif', block_vals, picked, preferred_element_type=jnp...]
  transfers between devices with their start and end apart: 5 -> 0, of which waited for: 5 -> 0; matrix products, arithmetic and copies ran while one was open for 16% -> 0% of each run, Pallas kernels for 0% -> 0%
where the time goes in v1:
time: 115 us; the launch traced here: 114 us
  Pallas kernels  103 us (90%)
  local copies, waits for them, and re-layouts  10.1 us (9%)
  between operations  1.31 us (1%)
    pallas_call x1, Pallas kernels, body(): pl.pallas_call(kernel, out_shape=(jax.ShapeDtypeStruct((256, FEAT), BF16)...  103 us
    unnamed x22, local copies, waits for them, and re-layouts  10.1 us

profile of v1, /device:TPU:1, one launch (start us, length us, event | category | flops | bytes accessed | tf_op | source)
XLA Modules:
  0.0 114.3 jit_solution(13859399733868753989)
XLA Ops:
  1.3 0.0 copy-start
  1.3 0.9 copy-done
  2.2 0.0 copy-start.1
  2.2 0.9 copy-done.1
  3.1 0.0 copy-start.2
  3.1 0.8 copy-done.2
  3.9 0.0 copy-start.3
  3.9 0.8 copy-done.3
  4.8 0.0 copy-start.4
  4.8 0.8 copy-done.4
  5.6 0.0 copy-start.5
  5.6 0.7 copy-done.5
  6.3 0.0 copy-start.6
  6.3 0.7 copy-done.6
  7.0 0.0 copy-start.7
  7.0 0.7 copy-done.7
  7.6 102.9 %layer.1 = (bf16[256,256]{1,0:T(8,128)(2,1)S(1)}, bf16[256,256]{1,0:T(8,128)(2,1)S(1)}, f32[256,128]{1,0:T(8,128)S(1)}, f32[256,128]{1,0:T(8,128)S(1)}, f32[128,256]{1,0:T(8,128)S(1)}, /*index=5*/f32[1,128]{1,0:T(1,128)S(1)}) custom-call(s32[1]{0:T(128)S(6)} %copy.22.used_ref, bf16[256,256]{1,0:T(8,128)(2,1)S(1)} %copy-done, ...), custom_call_target="tpu_custom_call" | custom-call | tf_op jit(solution)/shard_map/layer/pallas_call | solution.py:397
  110.6 0.7 copy.23
  111.2 0.7 copy.24
  111.9 0.7 copy.25
  112.5 0.7 copy.26
  113.2 0.7 copy.27
  113.8 0.5 copy.28
Async XLA Ops:
  1.3 0.9 copy-start
  2.2 0.9 copy-start.1
  3.1 0.8 copy-start.2
  3.9 0.8 copy-start.3
  4.8 0.8 copy-start.4
  5.6 0.7 copy-start.5
  6.3 0.7 copy-start.6
  7.0 0.7 copy-start.7

commit v2 on v1

v2 whole, which is shorter than its diff:
```python
import functools
import math

import jax
import jax.numpy as jnp
from jax import lax
from jax.experimental import pallas as pl
from jax.experimental.pallas import tpu as pltpu
from jax.sharding import PartitionSpec as P

FEAT = 256
HID = 128
TILE = 128
NBLK = 176
NB_PAD = 256
BROWS = 16
CTILES = 64
ZERO_SLOT = NBLK
MESH = pl.DeviceIdType.MESH
F32 = jnp.float32
BF16 = jnp.bfloat16
UNROLL = 8
CUT = 192
SELF_ROWS = 24
MSG_ROWS = 8


def dot(a, b, dims=((1,), (0,))):
    return lax.dot_general(a, b, (dims, ((), ())), preferred_element_type=F32)


def kernel(
    used_ref, x_hbm, values_ref, brow_hbm, bcol_hbm, ws_hbm, wm_hbm, bias_hbm, wo_hbm, cot_hbm,
    updated_hbm, gnodes_hbm, gself_hbm, gmsg_hbm, gout_hbm, gbias_hbm,
    updated_ref, gnodes_ref, gself_ref, gmsg_ref, gout_ref, gbias_ref,
    x_ref, brow_ref, bcol_ref, ws_ref, wm_ref, bias_ref, wo_ref, cot_ref,
    vals, gath, xgath, runs, idx_v, idx_s, ident, base, hgrad,
    part_send, recv_a, recv_b, zsend, recv_z, pgt,
    t_send, recv_c, t_sum, recv_ya, za_send, recv_za, recv_zb, yb_send, recv_yb,
    m_a, m_a_in, m_a_rep, m_a_fin, m_b, m_b_in, m_b_rep, m_b_fin,
    in_sems, out_sems, v_sem, i_sem, send_sems,
    p1za, p1ya, p1yb, p1zb, p1ca, p1cb, xgz, xgy,
    r3a, r3b, r3z, r5x, r5z, r5f, r7c, r7ya, r7za, r7zb, r7yb,
    aa_in, aa_rep, aa_out, ab_in, ab_rep, ab_out,
):
    row = lax.axis_index("rows")
    rep = lax.axis_index("rep")
    zl, y, c = row // 8, (row // 2) % 4, row % 2
    x, zh = rep // 2, rep % 2
    oc, ozh = 1 - c, 1 - zh

    def dev(zl_=None, y_=None, c_=None, x_=None, zh_=None):
        zl_ = zl if zl_ is None else zl_
        y_ = y if y_ is None else y_
        c_ = c if c_ is None else c_
        x_ = x if x_ is None else x_
        zh_ = zh if zh_ is None else zh_
        return {"rows": zl_ * 8 + y_ * 2 + c_, "rep": x_ * 2 + zh_}

    def around(i, d):
        return (i + d) % 4

    near = (1, 3, 2)
    sibling = dev(c_=oc)
    partner = dev(zh_=ozh)
    pairs = (
        (x_hbm, x_ref), (wm_hbm, wm_ref), (brow_hbm, brow_ref), (bcol_hbm, bcol_ref),
        (ws_hbm, ws_ref), (bias_hbm, bias_ref), (wo_hbm, wo_ref), (cot_hbm, cot_ref),
    )
    loads = [pltpu.make_async_copy(a, b, in_sems.at[i]) for i, (a, b) in enumerate(pairs)]
    for copy in loads:
        copy.start()
    partners = [partner, sibling]
    for d in near:
        partners += [dev(zl_=around(zl, d)), dev(y_=around(y, d)), dev(x_=around(x, d))]
    barrier = pltpu.get_barrier_semaphore()
    for p in partners:
        pl.semaphore_signal(barrier, inc=1, device_id=p, device_id_type=MESH)
    load_values = pltpu.make_async_copy(values_ref.at[0], vals, v_sem)
    load_values.start()

    sent = []

    def send(src, dst, recv, to):
        copy = pltpu.make_async_remote_copy(
            src_ref=src, dst_ref=dst, send_sem=send_sems.at[len(sent)], recv_sem=recv,
            device_id=to, device_id_type=MESH,
        )
        copy.start()
        sent.append(copy)

    def share(ref, recv, to):
        send(ref, ref, recv, to)

    def arrived(dst, recv):
        pltpu.make_async_remote_copy(
            src_ref=dst, dst_ref=dst, send_sem=send_sems.at[0], recv_sem=recv,
            device_id=sibling, device_id_type=MESH,
        ).wait_recv()

    def head(c_, zl_, y_):
        return gath.at[c_ * 4 + zl_, y_, pl.ds(0, 3)]

    def tail(c_, zl_, y_):
        return gath.at[c_ * 4 + zl_, y_, 3]

    def tails(c_, zl_):
        return gath.at[c_ * 4 + zl_, :, 3]

    loads[0].wait()
    loads[1].wait()
    feats = x_ref[...]
    gath[c * 4 + zl, y] = dot(feats, wm_ref[...]).astype(BF16).reshape(4, 64, HID)
    xgath[zl, y] = feats
    pl.semaphore_wait(barrier, len(partners))
    for d in near:
        share(head(c, zl, y), p1za.at[zl], dev(zl_=around(zl, d)))
    for d in near:
        share(tail(c, zl, y), p1yb.at[y], dev(y_=around(y, d)))
    for d in near:
        share(head(c, zl, y), p1ya.at[zl, y], dev(y_=around(y, d)))
    share(head(c, zl, y), p1ca.at[zl, y], sibling)

    for copy in loads[2:]:
        copy.wait()
    used = used_ref[0]
    idx_v[...] = jnp.zeros_like(idx_v)
    idx_v[0:1, 0:NBLK] = brow_ref[...]
    idx_v[1:2, 0:NBLK] = bcol_ref[...]
    lane = lax.broadcasted_iota(jnp.int32, (1, NB_PAD), 1)
    lanes = lax.broadcasted_iota(jnp.int32, (NB_PAD, NB_PAD), 1)
    usable = lane < used
    rows_of = idx_v[0:1, :]
    cols_of = idx_v[1:2, :]
    source = cols_of >> 1
    tile_of = (((source & 1) * 16 + (source >> 3) * 4 + ((source >> 1) & 3)) << 1) + (cols_of & 1)

    def listing(key, other):
        packed = (((key << 8) + lane) << 7) + other
        along = jnp.broadcast_to(packed, (NB_PAD, NB_PAD))
        down = along.T
        rank = jnp.sum((along < down).astype(jnp.int32), axis=1, keepdims=True)
        ordered = jnp.sum(jnp.where(rank == lanes, down, 0), axis=0, keepdims=True)
        keys = down >> 15
        upto = jnp.sum((keys <= lanes).astype(jnp.int32), axis=0, keepdims=True)
        below = jnp.sum((keys < lanes).astype(jnp.int32), axis=0, keepdims=True)
        return ordered, jnp.where(upto > below, upto - 1, ZERO_SLOT)

    def list_blocks():
        order_f, end_f = listing(jnp.where(usable, rows_of, BROWS), tile_of)
        order_b, end_b = listing(jnp.where(usable, tile_of, CTILES), rows_of)
        idx_v[0:1, :] = order_f
        idx_v[1:2, :] = end_f
        idx_v[2:3, :] = order_b
        idx_v[3:4, :] = end_b

    list_blocks()
    load_index = pltpu.make_async_copy(idx_v, idx_s, i_sem)
    load_index.start()

    def pass_head(d):
        zs = around(zl, d)
        arrived(head(c, zs, y), p1za.at[zs])
        for e in near:
            share(head(c, zs, y), p1ya.at[zs, y], dev(y_=around(y, e)))
        share(head(c, zs, y), p1ca.at[zs, y], sibling)

    pass_head(1)
    for e in near:
        ys = around(y, e)
        arrived(tail(c, zl, ys), p1yb.at[ys])
    for d in near:
        share(tails(c, zl), p1zb.at[zl], dev(zl_=around(zl, d)))
    share(tails(c, zl), p1cb.at[zl], sibling)
    pass_head(3)
    pass_head(2)

    ident[...] = dot(feats, ws_ref[...]) + bias_ref[...]
    cot = cot_ref[...]
    hgrad[...] = dot(cot, wo_ref[...], ((1,), (1,)))
    runs[ZERO_SLOT] = jnp.zeros((TILE, HID), F32)

    for d in (0,) + near:
        zs = around(zl, d)
        for e in near:
            ys = around(y, e)
            arrived(head(c, zs, ys), p1ya.at[zs, ys])
            share(head(c, zs, ys), p1ca.at[zs, ys], sibling)
        if d:
            arrived(tails(c, zs), p1zb.at[zs])
            share(tails(c, zs), p1cb.at[zs], sibling)
    for d in near:
        share(xgath.at[zl, y], xgz.at[zl], dev(zl_=around(zl, d)))
    load_values.wait()
    load_index.wait()
    for zs in range(4):
        arrived(tails(oc, zs), p1cb.at[zs])
        for ys in range(4):
            arrived(head(oc, zs, ys), p1ca.at[zs, ys])

    def products(which, pick):
        def step(i, carry):
            total, before = carry
            for u in range(UNROLL):
                p = i * UNROLL + u
                word = idx_s[which, p]
                key = word >> 15
                term = pick((word >> 7) & 255, word & 127)
                total = jnp.where(key == before, total, 0.0) + term
                runs[p] = total
                before = key
            return total, before

        lax.fori_loop(0, NBLK // UNROLL, step, (jnp.zeros((TILE, HID), F32), jnp.int32(-1)))

    def source_tile(o):
        a, b, q = o >> 3, (o >> 1) & 3, (o & 1) * 2
        return jnp.concatenate([gath[a, b, q], gath[a, b, q + 1]], axis=0)

    products(0, lambda b, o: dot(vals[b], source_tile(o)))

    def part(j, k):
        return runs[idx_s[1, j * 2 + k]]

    for zz, recv_sems, recv in ((ozh, r3a, recv_a), (zh, r3b, recv_b)):
        for k in range(2):
            for d in near:
                xs = around(x, d)
                j = xs * 2 + zz
                part_send[j, k] = part(j, k).astype(BF16)
                send(part_send.at[j, k], recv.at[x, k], recv_sems.at[x, k], dev(x_=xs))
    for d in near:
        zs = around(zl, d)
        arrived(xgath.at[zs, y], xgz.at[zs])
    for e in near:
        share(xgath.at[:, y], xgy.at[y], dev(y_=around(y, e)))

    def summed(recv, recv_sems, zz, k):
        total = part(x * 2 + zz, k)
        for d in near:
            xs = around(x, d)
            arrived(recv.at[xs, k], recv_sems.at[xs, k])
            total = total + recv[xs, k].astype(F32)
        return total

    for k in range(2):
        zsend[k] = summed(recv_a, r3a, ozh, k).astype(BF16)
        send(zsend.at[k], recv_z.at[k], r3z.at[k], partner)
    agg = [summed(recv_b, r3b, zh, k) for k in range(2)]
    hidden, pgrad = [], []
    for k in range(2):
        here = pl.ds(k * TILE, TILE)
        arrived(recv_z.at[k], r3z.at[k])
        pre = ident[here, :] + (agg[k] + recv_z[k].astype(F32))
        sig = jax.nn.sigmoid(pre)
        grad = hgrad[here, :] * sig * (1.0 + pre * (1.0 - sig))
        pgt[rep, k] = grad.T.astype(BF16)
        share(pgt.at[rep, k], r5z.at[k], partner)
        for d in near:
            share(pgt.at[rep, k], r5x.at[x, k], dev(x_=around(x, d)))
        hidden.append((pre * sig).astype(BF16))
        pgrad.append(grad.astype(BF16))

    hid = jnp.concatenate(hidden, axis=0)
    pg = jnp.concatenate(pgrad, axis=0)
    updated_ref[...] = (feats.astype(F32) + dot(hid, wo_ref[...])).astype(BF16)
    base[...] = cot.astype(F32) + dot(pg, ws_ref[...], ((1,), (1,)))
    term_self = dot(feats, pg, ((0,), (0,)))
    term_out = dot(hid, cot, ((0,), (0,)))
    term_bias = jnp.sum(pg.astype(F32).reshape(32, 8, HID), axis=0)
    m_a[:, 0:8, :] = term_self.reshape(32, 8, HID)
    m_a[0:16, 8:16, :] = term_out[:, 0:128].reshape(16, 8, HID)
    m_a[16:32, 8:16, :] = term_out[:, 128:256].reshape(16, 8, HID)
    m_a[:, 16:24, :] = jnp.broadcast_to(term_bias[None], (32, 8, HID))

    oj = x * 2 + ozh
    for k in range(2):
        arrived(pgt.at[oj, k], r5z.at[k])
        for d in near:
            share(pgt.at[oj, k], r5f.at[x, k], dev(x_=around(x, d)))
    for k in range(2):
        for d in near:
            xs = around(x, d)
            arrived(pgt.at[xs * 2 + zh, k], r5x.at[xs, k])
            arrived(pgt.at[xs * 2 + ozh, k], r5f.at[xs, k])

    spot = c * 16 + x * 4 + y
    level = zh * 4 + zl

    def plane():
        for cc in range(2):
            for a in range(4):
                for b in range(4):
                    if (cc, a, b) != (0, 0, 0):
                        ct, xt, yt = (c + cc) % 2, around(x, a), around(y, b)
                        yield ct * 16 + xt * 4 + yt, dev(c_=ct, x_=xt, y_=yt)

    def column_devices():
        for d in range(1, 8):
            z = (level + d) % 8
            yield z, dev(zl_=z % 4, zh_=z // 4)

    def grads_scatter(m, m_in, sem):
        m_in[spot] = m[spot]
        for q, to in plane():
            send(m.at[q], m_in.at[spot], sem.at[spot], to)

    def grads_level(m_in, m_rep, sem_in, sem):
        for q, _ in plane():
            arrived(m_in.at[q], sem_in.at[q])
        total = m_in[0]
        for q in range(1, 32):
            total = total + m_in[q]
        m_rep[level] = total
        for _, to in column_devices():
            share(m_rep.at[level], sem.at[level], to)

    def grads_spread(m_rep, m_fin, sem_rep, sem):
        for z, _ in column_devices():
            arrived(m_rep.at[z], sem_rep.at[z])
        total = m_rep[0]
        for z in range(1, 8):
            total = total + m_rep[z]
        m_fin[spot] = total
        for _, to in plane():
            share(m_fin.at[spot], sem.at[spot], to)

    def grads_end(m_fin, sem_out):
        for q, _ in plane():
            arrived(m_fin.at[q], sem_out.at[q])

    grads_scatter(m_a, m_a_in, aa_in)
    products(2, lambda b, o: dot(pgt[o >> 1, o & 1], vals[b]))

    def column(c_, zl_, y_, k):
        return runs[idx_s[3, ((c_ * 4 + zl_) * 4 + y_) * 2 + k]]

    for d in near + (0,):
        zs = around(zl, d)
        for ys in range(4):
            for k in range(2):
                t_send[zs, ys, k * TILE:(k + 1) * TILE, :] = column(oc, zs, ys, k).astype(BF16)
        send(t_send.at[zs], recv_c.at[zs], r7c.at[zs], sibling)
    grads_level(m_a_in, m_a_rep, aa_in, aa_rep)
    for d in near + (0,):
        zs = around(zl, d)
        arrived(recv_c.at[zs], r7c.at[zs])
        for ys in range(4):
            for k in range(2):
                here = slice(k * TILE, (k + 1) * TILE)
                total = column(c, zs, ys, k) + recv_c[zs, ys, here, :].astype(F32)
                t_sum[zs, ys, here, :] = total.astype(BF16)
        if d:
            send(t_sum.at[zs, :, pl.ds(CUT, 256 - CUT)], recv_zb.at[zl], r7zb.at[zl], dev(zl_=zs))
        for e in near:
            ys = around(y, e)
            send(t_sum.at[zs, ys, pl.ds(0, CUT)], recv_ya.at[y, zs], r7ya.at[y, zs], dev(y_=ys))

    for e in near:
        ys = around(y, e)
        arrived(xgath.at[:, ys], xgy.at[ys])

    def message(zs, total):
        for ys in range(4):
            both = jnp.concatenate([t_sum[zs, ys, 0:TILE, :], t_sum[zs, ys, TILE:256, :]], axis=1)
            total = total + dot(both, xgath[zs, ys])
        return total

    term_msg = lax.fori_loop(0, 4, message, jnp.zeros((HID, FEAT), F32))
    m_b[...] = term_msg.T.reshape(32, 8, HID)
    grads_scatter(m_b, m_b_in, ab_in)

    def heads(zs):
        total = t_sum[zs, y, 0:CUT, :].astype(F32)
        for e in near:
            ys = around(y, e)
            arrived(recv_ya.at[ys, zs], r7ya.at[ys, zs])
            total = total + recv_ya[ys, zs].astype(F32)
        return total

    for d in near:
        zs = around(zl, d)
        za_send[zs] = heads(zs).astype(BF16)
        send(za_send.at[zs], recv_za.at[zl], r7za.at[zl], dev(zl_=zs))
    for d in near:
        zs = around(zl, d)
        arrived(recv_zb.at[zs], r7zb.at[zs])
    for e in near + (0,):
        ys = around(y, e)
        final_b = t_sum[zl, ys, CUT:256, :].astype(F32)
        for d in near:
            final_b = final_b + recv_zb[around(zl, d), ys].astype(F32)
        if e:
            yb_send[ys] = final_b.astype(BF16)
            send(yb_send.at[ys], recv_yb.at[y], r7yb.at[y], dev(y_=ys))
    grads_spread(m_a_rep, m_a_fin, aa_rep, aa_out)
    grads_level(m_b_in, m_b_rep, ab_in, ab_rep)
    final_a = heads(zl)
    for d in near:
        zs = around(zl, d)
        arrived(recv_za.at[zs], r7za.at[zs])
        final_a = final_a + recv_za[zs].astype(F32)
    for e in near:
        ys = around(y, e)
        arrived(recv_yb.at[ys], r7yb.at[ys])
        final_b = final_b + recv_yb[ys].astype(F32)
    second = jnp.concatenate([final_a[TILE:CUT], final_b], axis=0)
    for k, total in enumerate((final_a[0:TILE], second)):
        here = pl.ds(k * TILE, TILE)
        gnodes_ref[here, :] = (
            base[here, :] + dot(total.T.astype(BF16), wm_ref[...], ((1,), (1,)))
        ).astype(BF16)
    stores = [
        pltpu.make_async_copy(a, b, out_sems.at[i])
        for i, (a, b) in enumerate((
            (updated_ref, updated_hbm), (gnodes_ref, gnodes_hbm), (gself_ref, gself_hbm),
            (gout_ref, gout_hbm), (gbias_ref, gbias_hbm), (gmsg_ref, gmsg_hbm),
        ))
    ]
    stores[0].start()
    stores[1].start()
    grads_spread(m_b_rep, m_b_fin, ab_rep, ab_out)
    grads_end(m_a_fin, aa_out)
    factor = 1.0 / math.sqrt(65536)
    gself_ref[...] = m_a_fin[:, 0:8, :].reshape(FEAT, HID) * factor
    gout_ref[:, 0:128] = m_a_fin[0:16, 8:16, :].reshape(HID, 128) * factor
    gout_ref[:, 128:256] = m_a_fin[16:32, 8:16, :].reshape(HID, 128) * factor
    gbias_ref[...] = jnp.sum(m_a_fin[0, 16:24, :], axis=0, keepdims=True) * factor
    for copy in stores[2:5]:
        copy.start()
    grads_end(m_b_fin, ab_out)
    gmsg_ref[...] = m_b_fin[...].reshape(FEAT, HID) * factor
    stores[5].start()
    for copy in sent:
        copy.wait_send()
    for copy in stores:
        copy.wait()


def write_out(*refs):
    ins, outs, held, sems = refs[:6], refs[6:12], refs[12:18], refs[18]
    loads = [pltpu.make_async_copy(ins[i], held[i], sems.at[0, i]) for i in range(6)]
    stores = [pltpu.make_async_copy(held[i], outs[i], sems.at[1, i]) for i in range(6)]
    for copy in loads:
        copy.start()
    for load, store in zip(loads, stores):
        load.wait()
        store.start()
    for copy in stores:
        copy.wait()


def body(x, values, brow, bcol, used, ws, wm, bias, wo, cot):
    dma = pltpu.SemaphoreType.DMA

    def pieces(n):
        return [pltpu.VMEM((m, n, HID), F32) for m in (32, 32, 8, 32)]

    out_shape = (
        jax.ShapeDtypeStruct((256, FEAT), BF16),
        jax.ShapeDtypeStruct((256, FEAT), BF16),
        jax.ShapeDtypeStruct((FEAT, HID), F32),
        jax.ShapeDtypeStruct((FEAT, HID), F32),
        jax.ShapeDtypeStruct((HID, FEAT), F32),
        jax.ShapeDtypeStruct((1, HID), F32),
    )
    hbm = pl.BlockSpec(memory_space=pltpu.HBM)
    results = pl.pallas_call(
        kernel,
        out_shape=out_shape,
        in_specs=[pl.BlockSpec(memory_space=pltpu.SMEM)] + [hbm] * 9,
        out_specs=(hbm,) * 6,
        scratch_shapes=[
            *[pltpu.VMEM(shape.shape, shape.dtype) for shape in out_shape],
            pltpu.VMEM((256, FEAT), BF16),
            pltpu.VMEM((1, NBLK), jnp.int32),
            pltpu.VMEM((1, NBLK), jnp.int32),
            pltpu.VMEM((FEAT, HID), BF16),
            pltpu.VMEM((FEAT, HID), BF16),
            pltpu.VMEM((1, HID), F32),
            pltpu.VMEM((HID, FEAT), BF16),
            pltpu.VMEM((256, FEAT), BF16),
            pltpu.VMEM((NBLK, TILE, TILE), BF16),
            pltpu.VMEM((8, 4, 4, 64, HID), BF16),
            pltpu.VMEM((4, 4, 256, FEAT), BF16),
            pltpu.VMEM((NBLK + 1, TILE, HID), F32),
            pltpu.VMEM((8, NB_PAD), jnp.int32),
            pltpu.SMEM((8, NB_PAD), jnp.int32),
            pltpu.VMEM((256, HID), F32),
            pltpu.VMEM((256, FEAT), F32),
            pltpu.VMEM((256, HID), F32),
            pltpu.VMEM((8, 2, TILE, HID), BF16),
            pltpu.VMEM((4, 2, TILE, HID), BF16),
            pltpu.VMEM((4, 2, TILE, HID), BF16),
            pltpu.VMEM((2, TILE, HID), BF16),
            pltpu.VMEM((2, TILE, HID), BF16),
            pltpu.VMEM((8, 2, HID, TILE), BF16),
            pltpu.VMEM((4, 4, 256, TILE), BF16),
            pltpu.VMEM((4, 4, 256, TILE), BF16),
            pltpu.VMEM((4, 4, 256, TILE), BF16),
            pltpu.VMEM((4, 4, CUT, TILE), BF16),
            pltpu.VMEM((4, CUT, TILE), BF16),
            pltpu.VMEM((4, CUT, TILE), BF16),
            pltpu.VMEM((4, 4, 256 - CUT, TILE), BF16),
            pltpu.VMEM((4, 256 - CUT, TILE), BF16),
            pltpu.VMEM((4, 256 - CUT, TILE), BF16),
            *pieces(SELF_ROWS),
            *pieces(MSG_ROWS),
            dma((8,)), dma((6,)), dma, dma, dma((280,)),
            dma((4,)), dma((4, 4)), dma((4,)), dma((4,)), dma((4, 4)), dma((4,)), dma((4,)), dma((4,)),
            dma((4, 2)), dma((4, 2)), dma((2,)), dma((4, 2)), dma((2,)), dma((4, 2)),
            dma((4,)), dma((4, 4)), dma((4,)), dma((4,)), dma((4,)),
            dma((32,)), dma((8,)), dma((32,)),
            dma((32,)), dma((8,)), dma((32,)),
        ],
        compiler_params=pltpu.CompilerParams(
            collective_id=0, has_side_effects=True, vmem_limit_bytes=63 * 2**20
        ),
        name="layer",
    )(used, x, values, brow, bcol, ws, wm, bias.reshape(1, HID), wo, cot)
    updated, gnodes, gself, gmsg, gout, gbias = pl.pallas_call(
        write_out,
        out_shape=out_shape,
        in_specs=[hbm] * 6,
        out_specs=(hbm,) * 6,
        scratch_shapes=[*[pltpu.VMEM(shape.shape, shape.dtype) for shape in out_shape], dma((2, 6))],
        name="write_out",
    )(*results)
    return updated, gnodes, gself, gmsg, gout, gbias.reshape(HID)


def solution(mesh):
    sharded = P(("rows", "rep"), None)
    in_specs = (
        sharded, P(("rows", "rep"), None, None, None), sharded, sharded, P(("rows", "rep")),
        P(), P(), P(), P(), sharded,
    )
    out_specs = (sharded, sharded, P(), P(), P(), P())
    return jax.shard_map(body, mesh=mesh, in_specs=in_specs, out_specs=out_specs, check_vma=False)
```

time: 115 us -> 93.8 us (0.82)
  Pallas kernels: 103 us -> 92.4 us
  local copies, waits for them, and re-layouts: 10.1 us -> 0 us
    pallas_call x1 -> x2, Pallas kernels: 103 us -> 92.4 us  [the longest x1 90.4 us: body(): pl.pallas_call(kernel, out_shape=out_shape, in_specs=[pl.BlockSpec(memory...]
    unnamed x22 -> x0, local copies, waits for them, and re-layouts: 10.1 us -> none
where the time goes in v2:
time: 93.8 us; the launch traced here: 93.7 us
  Pallas kernels  92.4 us (99%)
  between operations  1.29 us (1%)
    pallas_call x1, Pallas kernels, body(): pl.pallas_call(kernel, out_shape=out_shape, in_specs=[pl.BlockSpec(memory...  90.4 us
    pallas_call x1, Pallas kernels, body(): pl.pallas_call(write_out, out_shape=out_shape, in_specs=[hbm] * 6, out_sp...  1.93 us

profile of v2, /device:TPU:1, one launch (start us, length us, event | category | flops | bytes accessed | tf_op | source)
XLA Modules:
  0.0 93.7 jit_solution(17447670771194131683)
XLA Ops:
  1.3 90.4 %layer.1 = (bf16[256,256]{1,0:T(8,128)(2,1)}, bf16[256,256]{1,0:T(8,128)(2,1)}, f32[256,128]{1,0:T(8,128)}, f32[256,128]{1,0:T(8,128)}, f32[128,256]{1,0:T(8,128)}, /*index=5*/f32[1,128]{1,0:T(1,128)}) custom-call(s32[1]{0:T(128)S(6)} %copy.16.used_ref, bf16[256,256]{1,0:T(8,128)(2,1)} %x_hbm.1, bf16[1,176,128,128]{3,2,1,0:T(8,128)(2,1)} %values_ref.1, ...), custom_call_target="tpu_custom_call" | custom-call | tf_op jit(solution)/shard_map/layer/pallas_call | solution.py:468
  91.7 1.9 %write_out.1 = (bf16[256,256]{1,0:T(8,128)(2,1)}, bf16[256,256]{1,0:T(8,128)(2,1)}, f32[256,128]{1,0:T(8,128)}, f32[256,128]{1,0:T(8,128)}, f32[128,256]{1,0:T(8,128)}, /*index=5*/f32[1,128]{1,0:T(1,128)}) custom-call(bf16[256,256]{1,0:T(8,128)(2,1)} %get-tuple-element.18.refs_0_, bf16[256,256]{1,0:T(8,128)(2,1)} %get-tuple-element.19.refs_1_, ...), custom_call_target="tpu_custom_call" | custom-call | tf_op jit(solution)/shard_map/write_out/pallas_call | solution.py:521

commit v3 on v2

--- a/solution.py
+++ b/solution.py
@@ -19,10 +19,8 @@
 MESH = pl.DeviceIdType.MESH
 F32 = jnp.float32
 BF16 = jnp.bfloat16
-UNROLL = 8
+UNROLL = 44
 CUT = 192
-SELF_ROWS = 24
-MSG_ROWS = 8
 
 
 def dot(a, b, dims=((1,), (0,))):
@@ -37,11 +35,11 @@
     vals, gath, xgath, runs, idx_v, idx_s, ident, base, hgrad,
     part_send, recv_a, recv_b, zsend, recv_z, pgt,
     t_send, recv_c, t_sum, recv_ya, za_send, recv_za, recv_zb, yb_send, recv_yb,
-    m_a, m_a_in, m_a_rep, m_a_fin, m_b, m_b_in, m_b_rep, m_b_fin,
+    m_a, a_core, a_y, a_x, m_a_rep, m_a_fin, m_b, m_b_in, m_b_rep, m_b_fin,
     in_sems, out_sems, v_sem, i_sem, send_sems,
     p1za, p1ya, p1yb, p1zb, p1ca, p1cb, xgz, xgy,
     r3a, r3b, r3z, r5x, r5z, r5f, r7c, r7ya, r7za, r7zb, r7yb,
-    aa_in, aa_rep, aa_out, ab_in, ab_rep, ab_out,
+    aa_c, aa_y, aa_x, aa_z, aa_ox, aa_oy, aa_oc, ab_in, ab_rep, ab_out,
 ):
     row = lax.axis_index("rows")
     rep = lax.axis_index("rep")
@@ -174,6 +172,8 @@
     share(tails(c, zl), p1cb.at[zl], sibling)
     pass_head(3)
     pass_head(2)
+    for d in near:
+        share(xgath.at[zl, y], xgz.at[zl], dev(zl_=around(zl, d)))
 
     ident[...] = dot(feats, ws_ref[...]) + bias_ref[...]
     cot = cot_ref[...]
@@ -189,14 +189,22 @@
         if d:
             arrived(tails(c, zs), p1zb.at[zs])
             share(tails(c, zs), p1cb.at[zs], sibling)
-    for d in near:
-        share(xgath.at[zl, y], xgz.at[zl], dev(zl_=around(zl, d)))
     load_values.wait()
     load_index.wait()
     for zs in range(4):
         arrived(tails(oc, zs), p1cb.at[zs])
         for ys in range(4):
             arrived(head(oc, zs, ys), p1ca.at[zs, ys])
+
+    def pass_raw(steps):
+        for d in steps:
+            zs = around(zl, d)
+            if d:
+                arrived(xgath.at[zs, y], xgz.at[zs])
+            for e in near:
+                share(xgath.at[zs, y], xgy.at[zs, y], dev(y_=around(y, e)))
+
+    pass_raw((0,))
 
     def products(which, pick):
         def step(i, carry):
@@ -229,11 +237,8 @@
                 j = xs * 2 + zz
                 part_send[j, k] = part(j, k).astype(BF16)
                 send(part_send.at[j, k], recv.at[x, k], recv_sems.at[x, k], dev(x_=xs))
-    for d in near:
-        zs = around(zl, d)
-        arrived(xgath.at[zs, y], xgz.at[zs])
-    for e in near:
-        share(xgath.at[:, y], xgy.at[y], dev(y_=around(y, e)))
+
+    pass_raw((1, 3))
 
     def summed(recv, recv_sems, zz, k):
         total = part(x * 2 + zz, k)
@@ -246,6 +251,7 @@
     for k in range(2):
         zsend[k] = summed(recv_a, r3a, ozh, k).astype(BF16)
         send(zsend.at[k], recv_z.at[k], r3z.at[k], partner)
+    pass_raw((2,))
     agg = [summed(recv_b, r3b, zh, k) for k in range(2)]
     hidden, pgrad = [], []
     for k in range(2):
@@ -268,35 +274,30 @@
     term_self = dot(feats, pg, ((0,), (0,)))
     term_out = dot(hid, cot, ((0,), (0,)))
     term_bias = jnp.sum(pg.astype(F32).reshape(32, 8, HID), axis=0)
-    m_a[:, 0:8, :] = term_self.reshape(32, 8, HID)
-    m_a[0:16, 8:16, :] = term_out[:, 0:128].reshape(16, 8, HID)
-    m_a[16:32, 8:16, :] = term_out[:, 128:256].reshape(16, 8, HID)
-    m_a[:, 16:24, :] = jnp.broadcast_to(term_bias[None], (32, 8, HID))
+    for h in range(2):
+        m_a[h, :, :, 0:8, :] = term_self[h * 128:(h + 1) * 128, :].reshape(4, 4, 8, HID)
+        m_a[h, :, :, 8:16, :] = term_out[:, h * 128:(h + 1) * 128].reshape(4, 4, 8, HID)
+        m_a[h, :, :, 16:24, :] = jnp.broadcast_to(term_bias[None, None], (4, 4, 8, HID))
+    send(m_a.at[oc], a_core, aa_c.at[0], sibling)
 
     oj = x * 2 + ozh
     for k in range(2):
         arrived(pgt.at[oj, k], r5z.at[k])
         for d in near:
             share(pgt.at[oj, k], r5f.at[x, k], dev(x_=around(x, d)))
-    for k in range(2):
-        for d in near:
-            xs = around(x, d)
-            arrived(pgt.at[xs * 2 + zh, k], r5x.at[xs, k])
-            arrived(pgt.at[xs * 2 + ozh, k], r5f.at[xs, k])
-
     spot = c * 16 + x * 4 + y
     level = zh * 4 + zl
 
     def plane():
-        for cc in range(2):
-            for a in range(4):
-                for b in range(4):
+        for a in (2, 1, 3, 0):
+            for b in (2, 1, 3, 0):
+                for cc in (1, 0):
                     if (cc, a, b) != (0, 0, 0):
                         ct, xt, yt = (c + cc) % 2, around(x, a), around(y, b)
                         yield ct * 16 + xt * 4 + yt, dev(c_=ct, x_=xt, y_=yt)
 
     def column_devices():
-        for d in range(1, 8):
+        for d in (4, 3, 5, 2, 6, 1, 7):
             z = (level + d) % 8
             yield z, dev(zl_=z % 4, zh_=z // 4)
 
@@ -329,8 +330,66 @@
         for q, _ in plane():
             arrived(m_fin.at[q], sem_out.at[q])
 
-    grads_scatter(m_a, m_a_in, aa_in)
+    def sums_x():
+        arrived(a_core, aa_c.at[0])
+        a_core[...] = a_core[...] + m_a[c]
+        for d in near:
+            xs = around(x, d)
+            send(a_core.at[xs], a_x.at[x], aa_x.at[x], dev(x_=xs))
+
+    def sums_y():
+        total = a_core[x]
+        for d in near:
+            xs = around(x, d)
+            arrived(a_x.at[xs], aa_x.at[xs])
+            total = total + a_x[xs]
+        a_x[x] = total
+        for d in near:
+            ys = around(y, d)
+            send(a_x.at[x, ys], a_y.at[y], aa_y.at[y], dev(y_=ys))
+
+    def sums_z():
+        total = a_x[x, y]
+        for d in near:
+            ys = around(y, d)
+            arrived(a_y.at[ys], aa_y.at[ys])
+            total = total + a_y[ys]
+        m_a_rep[level] = total
+        for _, to in column_devices():
+            share(m_a_rep.at[level], aa_z.at[level], to)
+
+    def spread_x():
+        for z, _ in column_devices():
+            arrived(m_a_rep.at[z], aa_z.at[z])
+        total = m_a_rep[0]
+        for z in range(1, 8):
+            total = total + m_a_rep[z]
+        m_a_fin[c, x, y] = total
+        for d in near:
+            share(m_a_fin.at[c, x, y], aa_ox.at[x], dev(x_=around(x, d)))
+
+    def spread_y():
+        for d in near:
+            xs = around(x, d)
+            arrived(m_a_fin.at[c, xs, y], aa_ox.at[xs])
+        for d in near:
+            share(m_a_fin.at[c, :, y], aa_oy.at[y], dev(y_=around(y, d)))
+
+    def spread_core():
+        for d in near:
+            ys = around(y, d)
+            arrived(m_a_fin.at[c, :, ys], aa_oy.at[ys])
+        share(m_a_fin.at[c], aa_oc.at[0], sibling)
+
+    sums_x()
+    for k in range(2):
+        for d in near:
+            xs = around(x, d)
+            arrived(pgt.at[xs * 2 + zh, k], r5x.at[xs, k])
+            arrived(pgt.at[xs * 2 + ozh, k], r5f.at[xs, k])
+    sums_y()
     products(2, lambda b, o: dot(pgt[o >> 1, o & 1], vals[b]))
+    sums_z()
 
     def column(c_, zl_, y_, k):
         return runs[idx_s[3, ((c_ * 4 + zl_) * 4 + y_) * 2 + k]]
@@ -341,7 +400,11 @@
             for k in range(2):
                 t_send[zs, ys, k * TILE:(k + 1) * TILE, :] = column(oc, zs, ys, k).astype(BF16)
         send(t_send.at[zs], recv_c.at[zs], r7c.at[zs], sibling)
-    grads_level(m_a_in, m_a_rep, aa_in, aa_rep)
+    def send_heads(zs):
+        for e in near:
+            ys = around(y, e)
+            send(t_sum.at[zs, ys, pl.ds(0, CUT)], recv_ya.at[y, zs], r7ya.at[y, zs], dev(y_=ys))
+
     for d in near + (0,):
         zs = around(zl, d)
         arrived(recv_c.at[zs], r7c.at[zs])
@@ -352,13 +415,13 @@
                 t_sum[zs, ys, here, :] = total.astype(BF16)
         if d:
             send(t_sum.at[zs, :, pl.ds(CUT, 256 - CUT)], recv_zb.at[zl], r7zb.at[zl], dev(zl_=zs))
-        for e in near:
-            ys = around(y, e)
-            send(t_sum.at[zs, ys, pl.ds(0, CUT)], recv_ya.at[y, zs], r7ya.at[y, zs], dev(y_=ys))
+        if d in (1, 3):
+            send_heads(zs)
 
     for e in near:
         ys = around(y, e)
-        arrived(xgath.at[:, ys], xgy.at[ys])
+        for zs in range(4):
+            arrived(xgath.at[zs, ys], xgy.at[zs, ys])
 
     def message(zs, total):
         for ys in range(4):
@@ -369,6 +432,9 @@
     term_msg = lax.fori_loop(0, 4, message, jnp.zeros((HID, FEAT), F32))
     m_b[...] = term_msg.T.reshape(32, 8, HID)
     grads_scatter(m_b, m_b_in, ab_in)
+    for d in (2, 0):
+        send_heads(around(zl, d))
+    spread_x()
 
     def heads(zs):
         total = t_sum[zs, y, 0:CUT, :].astype(F32)
@@ -382,6 +448,8 @@
         zs = around(zl, d)
         za_send[zs] = heads(zs).astype(BF16)
         send(za_send.at[zs], recv_za.at[zl], r7za.at[zl], dev(zl_=zs))
+    spread_y()
+    grads_level(m_b_in, m_b_rep, ab_in, ab_rep)
     for d in near:
         zs = around(zl, d)
         arrived(recv_zb.at[zs], r7zb.at[zs])
@@ -393,8 +461,7 @@
         if e:
             yb_send[ys] = final_b.astype(BF16)
             send(yb_send.at[ys], recv_yb.at[y], r7yb.at[y], dev(y_=ys))
-    grads_spread(m_a_rep, m_a_fin, aa_rep, aa_out)
-    grads_level(m_b_in, m_b_rep, ab_in, ab_rep)
+    spread_core()
     final_a = heads(zl)
     for d in near:
         zs = around(zl, d)
@@ -404,6 +471,7 @@
         ys = around(y, e)
         arrived(recv_yb.at[ys], r7yb.at[ys])
         final_b = final_b + recv_yb[ys].astype(F32)
+    grads_spread(m_b_rep, m_b_fin, ab_rep, ab_out)
     second = jnp.concatenate([final_a[TILE:CUT], final_b], axis=0)
     for k, total in enumerate((final_a[0:TILE], second)):
         here = pl.ds(k * TILE, TILE)
@@ -419,13 +487,13 @@
     ]
     stores[0].start()
     stores[1].start()
-    grads_spread(m_b_rep, m_b_fin, ab_rep, ab_out)
-    grads_end(m_a_fin, aa_out)
+    arrived(m_a_fin.at[oc], aa_oc.at[0])
     factor = 1.0 / math.sqrt(65536)
-    gself_ref[...] = m_a_fin[:, 0:8, :].reshape(FEAT, HID) * factor
-    gout_ref[:, 0:128] = m_a_fin[0:16, 8:16, :].reshape(HID, 128) * factor
-    gout_ref[:, 128:256] = m_a_fin[16:32, 8:16, :].reshape(HID, 128) * factor
-    gbias_ref[...] = jnp.sum(m_a_fin[0, 16:24, :], axis=0, keepdims=True) * factor
+    for h in range(2):
+        half = slice(h * 128, (h + 1) * 128)
+        gself_ref[half, :] = m_a_fin[h, :, :, 0:8, :].reshape(128, HID) * factor
+        gout_ref[:, half] = m_a_fin[h, :, :, 8:16, :].reshape(HID, 128) * factor
+    gbias_ref[...] = jnp.sum(m_a_fin[0, 0, 0, 16:24, :], axis=0, keepdims=True) * factor
     for copy in stores[2:5]:
         copy.start()
     grads_end(m_b_fin, ab_out)
@@ -452,9 +520,6 @@
 
 def body(x, values, brow, bcol, used, ws, wm, bias, wo, cot):
     dma = pltpu.SemaphoreType.DMA
-
-    def pieces(n):
-        return [pltpu.VMEM((m, n, HID), F32) for m in (32, 32, 8, 32)]
 
     out_shape = (
         jax.ShapeDtypeStruct((256, FEAT), BF16),
@@ -504,13 +569,13 @@
             pltpu.VMEM((4, 4, 256 - CUT, TILE), BF16),
             pltpu.VMEM((4, 256 - CUT, TILE), BF16),
             pltpu.VMEM((4, 256 - CUT, TILE), BF16),
-            *pieces(SELF_ROWS),
-            *pieces(MSG_ROWS),
+            *[pltpu.VMEM((*lead, 24, HID), F32) for lead in ((2, 4, 4), (4, 4), (4,), (4, 4), (8,), (2, 4, 4))],
+            *[pltpu.VMEM((lead, 8, HID), F32) for lead in (32, 32, 8, 32)],
             dma((8,)), dma((6,)), dma, dma, dma((280,)),
-            dma((4,)), dma((4, 4)), dma((4,)), dma((4,)), dma((4, 4)), dma((4,)), dma((4,)), dma((4,)),
+            dma((4,)), dma((4, 4)), dma((4,)), dma((4,)), dma((4, 4)), dma((4,)), dma((4,)), dma((4, 4)),
             dma((4, 2)), dma((4, 2)), dma((2,)), dma((4, 2)), dma((2,)), dma((4, 2)),
             dma((4,)), dma((4, 4)), dma((4,)), dma((4,)), dma((4,)),
-            dma((32,)), dma((8,)), dma((32,)),
+            dma((1,)), dma((4,)), dma((4,)), dma((8,)), dma((4,)), dma((4,)), dma((1,)),
             dma((32,)), dma((8,)), dma((32,)),
         ],
         compiler_params=pltpu.CompilerParams(

time: 93.8 us -> 85 us (0.906)
  Pallas kernels: 92.4 us -> 83.6 us
    pallas_call x1, Pallas kernels: 90.4 us -> 81.7 us  [body(): pl.pallas_call(kernel, out_shape=out_shape, in_specs=[pl.BlockSpec(memory...]
where the time goes in v3:
time: 85 us; the launch traced here: 84.9 us
  Pallas kernels  83.6 us (98%)
  between operations  1.29 us (2%)
    pallas_call x1, Pallas kernels, body(): pl.pallas_call(kernel, out_shape=out_shape, in_specs=[pl.BlockSpec(memory...  81.7 us
    pallas_call x1, Pallas kernels, body(): pl.pallas_call(write_out, out_shape=out_shape, in_specs=[hbm] * 6, out_sp...  1.93 us

profile of v3, /device:TPU:1, one launch (start us, length us, event | category | flops | bytes accessed | tf_op | source)
XLA Modules:
  0.0 84.9 jit_solution(3290360420842840879)
XLA Ops:
  1.3 81.7 %layer.1 = (bf16[256,256]{1,0:T(8,128)(2,1)}, bf16[256,256]{1,0:T(8,128)(2,1)}, f32[256,128]{1,0:T(8,128)}, f32[256,128]{1,0:T(8,128)}, f32[128,256]{1,0:T(8,128)}, /*index=5*/f32[1,128]{1,0:T(1,128)}) custom-call(s32[1]{0:T(128)S(6)} %copy.16.used_ref, bf16[256,256]{1,0:T(8,128)(2,1)} %x_hbm.1, bf16[1,176,128,128]{3,2,1,0:T(8,128)(2,1)} %values_ref.1, ...), custom_call_target="tpu_custom_call" | custom-call | tf_op jit(solution)/shard_map/layer/pallas_call | solution.py:533
  83.0 1.9 %write_out.1 = (bf16[256,256]{1,0:T(8,128)(2,1)}, bf16[256,256]{1,0:T(8,128)(2,1)}, f32[256,128]{1,0:T(8,128)}, f32[256,128]{1,0:T(8,128)}, f32[128,256]{1,0:T(8,128)}, /*index=5*/f32[1,128]{1,0:T(1,128)}) custom-call(bf16[256,256]{1,0:T(8,128)(2,1)} %get-tuple-element.18.refs_0_, bf16[256,256]{1,0:T(8,128)(2,1)} %get-tuple-element.19.refs_1_, ...), custom_call_target="tpu_custom_call" | custom-call | tf_op jit(solution)/shard_map/write_out/pallas_call | solution.py:586

commit v4 on v3

--- a/solution.py
+++ b/solution.py
@@ -172,8 +172,6 @@
     share(tails(c, zl), p1cb.at[zl], sibling)
     pass_head(3)
     pass_head(2)
-    for d in near:
-        share(xgath.at[zl, y], xgz.at[zl], dev(zl_=around(zl, d)))
 
     ident[...] = dot(feats, ws_ref[...]) + bias_ref[...]
     cot = cot_ref[...]
@@ -204,6 +202,8 @@
             for e in near:
                 share(xgath.at[zs, y], xgy.at[zs, y], dev(y_=around(y, e)))
 
+    for d in near:
+        share(xgath.at[zl, y], xgz.at[zl], dev(zl_=around(zl, d)))
     pass_raw((0,))
 
     def products(which, pick):
@@ -238,8 +238,6 @@
                 part_send[j, k] = part(j, k).astype(BF16)
                 send(part_send.at[j, k], recv.at[x, k], recv_sems.at[x, k], dev(x_=xs))
 
-    pass_raw((1, 3))
-
     def summed(recv, recv_sems, zz, k):
         total = part(x * 2 + zz, k)
         for d in near:
@@ -251,7 +249,7 @@
     for k in range(2):
         zsend[k] = summed(recv_a, r3a, ozh, k).astype(BF16)
         send(zsend.at[k], recv_z.at[k], r3z.at[k], partner)
-    pass_raw((2,))
+    pass_raw((1, 3))
     agg = [summed(recv_b, r3b, zh, k) for k in range(2)]
     hidden, pgrad = [], []
     for k in range(2):
@@ -267,6 +265,7 @@
         hidden.append((pre * sig).astype(BF16))
         pgrad.append(grad.astype(BF16))
 
+    pass_raw((2,))
     hid = jnp.concatenate(hidden, axis=0)
     pg = jnp.concatenate(pgrad, axis=0)
     updated_ref[...] = (feats.astype(F32) + dot(hid, wo_ref[...])).astype(BF16)

time: 85 us -> 84 us (0.988)
  Pallas kernels: 83.6 us -> 82.6 us
    pallas_call x1, Pallas kernels: 81.7 us -> 80.6 us  [body(): pl.pallas_call(kernel, out_shape=out_shape, in_specs=[pl.BlockSpec(memory...]
where the time goes in v4:
time: 84 us; the launch traced here: 83.8 us
  Pallas kernels  82.6 us (98%)
  between operations  1.29 us (2%)
    pallas_call x1, Pallas kernels, body(): pl.pallas_call(kernel, out_shape=out_shape, in_specs=[pl.BlockSpec(memory...  80.6 us
    pallas_call x1, Pallas kernels, body(): pl.pallas_call(write_out, out_shape=out_shape, in_specs=[hbm] * 6, out_sp...  1.93 us

profile of v4, /device:TPU:1, one launch (start us, length us, event | category | flops | bytes accessed | tf_op | source)
XLA Modules:
  0.0 83.8 jit_solution(16967551755859408162)
XLA Ops:
  1.3 80.6 %layer.1 = (bf16[256,256]{1,0:T(8,128)(2,1)}, bf16[256,256]{1,0:T(8,128)(2,1)}, f32[256,128]{1,0:T(8,128)}, f32[256,128]{1,0:T(8,128)}, f32[128,256]{1,0:T(8,128)}, /*index=5*/f32[1,128]{1,0:T(1,128)}) custom-call(s32[1]{0:T(128)S(6)} %copy.16.used_ref, bf16[256,256]{1,0:T(8,128)(2,1)} %x_hbm.1, bf16[1,176,128,128]{3,2,1,0:T(8,128)(2,1)} %values_ref.1, ...), custom_call_target="tpu_custom_call" | custom-call | tf_op jit(solution)/shard_map/layer/pallas_call | solution.py:532
  81.9 1.9 %write_out.1 = (bf16[256,256]{1,0:T(8,128)(2,1)}, bf16[256,256]{1,0:T(8,128)(2,1)}, f32[256,128]{1,0:T(8,128)}, f32[256,128]{1,0:T(8,128)}, f32[128,256]{1,0:T(8,128)}, /*index=5*/f32[1,128]{1,0:T(1,128)}) custom-call(bf16[256,256]{1,0:T(8,128)(2,1)} %get-tuple-element.18.refs_0_, bf16[256,256]{1,0:T(8,128)(2,1)} %get-tuple-element.19.refs_1_, ...), custom_call_target="tpu_custom_call" | custom-call | tf_op jit(solution)/shard_map/write_out/pallas_call | solution.py:585

commit v5 on v4

--- a/solution.py
+++ b/solution.py
@@ -404,6 +404,7 @@
             ys = around(y, e)
             send(t_sum.at[zs, ys, pl.ds(0, CUT)], recv_ya.at[y, zs], r7ya.at[y, zs], dev(y_=ys))
 
+    term_msg = jnp.zeros((HID, FEAT), F32)
     for d in near + (0,):
         zs = around(zl, d)
         arrived(recv_c.at[zs], r7c.at[zs])
@@ -416,19 +417,14 @@
             send(t_sum.at[zs, :, pl.ds(CUT, 256 - CUT)], recv_zb.at[zl], r7zb.at[zl], dev(zl_=zs))
         if d in (1, 3):
             send_heads(zs)
-
-    for e in near:
-        ys = around(y, e)
-        for zs in range(4):
+        for e in near:
+            ys = around(y, e)
             arrived(xgath.at[zs, ys], xgy.at[zs, ys])
-
-    def message(zs, total):
         for ys in range(4):
             both = jnp.concatenate([t_sum[zs, ys, 0:TILE, :], t_sum[zs, ys, TILE:256, :]], axis=1)
-            total = total + dot(both, xgath[zs, ys])
-        return total
-
-    term_msg = lax.fori_loop(0, 4, message, jnp.zeros((HID, FEAT), F32))
+            term_msg = term_msg + dot(both, xgath[zs, ys])
+
+
     m_b[...] = term_msg.T.reshape(32, 8, HID)
     grads_scatter(m_b, m_b_in, ab_in)
     for d in (2, 0):

time: 84 us -> 84 us (level)
  no operation moved by 1% of the time
where the time goes in v5:
time: 84 us; the launch traced here: 83.8 us
  Pallas kernels  82.6 us (98%)
  between operations  1.29 us (2%)
    pallas_call x1, Pallas kernels, body(): pl.pallas_call(kernel, out_shape=out_shape, in_specs=[pl.BlockSpec(memory...  80.6 us
    pallas_call x1, Pallas kernels, body(): pl.pallas_call(write_out, out_shape=out_shape, in_specs=[hbm] * 6, out_sp...  1.93 us

profile of v5, /device:TPU:1, one launch (start us, length us, event | category | flops | bytes accessed | tf_op | source)
XLA Modules:
  0.0 83.8 jit_solution(5480078350431861368)
XLA Ops:
  1.3 80.6 %layer.1 = (bf16[256,256]{1,0:T(8,128)(2,1)}, bf16[256,256]{1,0:T(8,128)(2,1)}, f32[256,128]{1,0:T(8,128)}, f32[256,128]{1,0:T(8,128)}, f32[128,256]{1,0:T(8,128)}, /*index=5*/f32[1,128]{1,0:T(1,128)}) custom-call(s32[1]{0:T(128)S(6)} %copy.16.used_ref, bf16[256,256]{1,0:T(8,128)(2,1)} %x_hbm.1, bf16[1,176,128,128]{3,2,1,0:T(8,128)(2,1)} %values_ref.1, ...), custom_call_target="tpu_custom_call" | custom-call | tf_op jit(solution)/shard_map/layer/pallas_call | solution.py:528
  81.9 1.9 %write_out.1 = (bf16[256,256]{1,0:T(8,128)(2,1)}, bf16[256,256]{1,0:T(8,128)(2,1)}, f32[256,128]{1,0:T(8,128)}, f32[256,128]{1,0:T(8,128)}, f32[128,256]{1,0:T(8,128)}, /*index=5*/f32[1,128]{1,0:T(1,128)}) custom-call(bf16[256,256]{1,0:T(8,128)(2,1)} %get-tuple-element.18.refs_0_, bf16[256,256]{1,0:T(8,128)(2,1)} %get-tuple-element.19.refs_1_, ...), custom_call_target="tpu_custom_call" | custom-call | tf_op jit(solution)/shard_map/write_out/pallas_call | solution.py:581
